TPU v7x, 32 devices: a whole 2x2x4 slice. The times are simulated.
32 devices in a mesh: groups: 2 (over x), ctx: 8 (over z, y), heads: 2 (over core).
Axes of the slice: x: 2, y: 2, z: 4, core: 2. Of those that a mesh axis runs over, the one named last changes fastest.
Arguments:
- query_vectors: bfloat16 [2048, 16, 128], P(('groups', 'ctx'), 'heads'), parts along dimension 0, may hold values from -5.5 to 5.5
- key_vectors: bfloat16 [2048, 4, 128], P(('groups', 'ctx'), 'heads'), parts along dimension 0, may hold values from -5.5 to 5.5
- value_rows: bfloat16 [2048, 4, 128], P(('groups', 'ctx'), 'heads'), parts along dimension 0, may hold values from -6 to 6
- forward_out: bfloat16 [2048, 16, 128], P(('groups', 'ctx'), 'heads'), parts along dimension 0, may hold values from -3 to 3
- out_grad: bfloat16 [2048, 16, 128], P(('groups', 'ctx'), 'heads'), parts along dimension 0, may hold values from -24 to 24
- block_offsets: int32 [16], P(('groups', 'ctx')), parts along dimension 0, may hold values from 0 to 7, each once
Outputs:
- query_grad: float32 [2048, 16, 128], P(('groups', 'ctx'), 'heads'), parts along dimension 0
- key_gradient_array: float32 [2048, 4, 128], P(('groups', 'ctx'), 'heads'), parts along dimension 0
- value_gradient_array: float32 [2048, 4, 128], P(('groups', 'ctx'), 'heads'), parts along dimension 0
There are 2 independent parts, one for each index of `groups`. A program takes and returns all parts, laid end to end along the dimension named above; each array names one. Nothing has to cross between parts.
Inputs may be any that keep to these rules, and one draw needn't show every extreme that they name: block_offsets is a permutation of 0 to 7.
All inputs are finite; a program needn't handle non-finite values.
Results may differ from a plain program's by a relative error of at most 0.0029.
Values may be sent and summed in bfloat16 or wider, within the bound.
A program may use at most 64 MiB of HBM per device.

v0:
```python
import functools

import jax
import jax.numpy as jnp
from jax import lax
from jax.experimental import pallas as pl
from jax.experimental.pallas import tpu as pltpu
from jax.sharding import PartitionSpec as P

MESH = pl.DeviceIdType.MESH
LOG2E = 1.4426950408889634
F32 = jnp.float32
BF16 = jnp.bfloat16
PAD = 16


def dot_nt(a, b):
    return lax.dot_general(a, b, (((1,), (1,)), ((), ())), preferred_element_type=F32)


def dot_nn(a, b):
    return lax.dot_general(a, b, (((1,), (0,)), ((), ())), preferred_element_type=F32)


def loop(n, body):
    if n <= 4:
        for i in range(n):
            body(i)
    else:
        def step(i, carry):
            body(i)
            return carry
        lax.fori_loop(0, n, step, 0)


def kernel(Z, Y, G, H, T, D, *refs):
    (q_hbm, k_hbm, v_hbm, fo_hbm, do_hbm, off_ref, dq_ref, dk_ref, dv_ref,
     q_ref, k_ref, v_ref, fo_ref, do_ref, in_sem,
     tmp, qs, dos, qst, dost, kst, vst, delta, delst, kbuf, vbuf,
     s_scr, ds_scr, top_scr, partv, partk,
     gsv, grv, gsk, grk,
     dqst, dqr, gst, gr, ys, yr,
     ks_s, ks_r, vs_s, vs_r, gv_s, gv_r, gk_s, gk_r) = refs
    me = lax.axis_index("ctx")
    z, y = me // Y, me % Y
    other = 1 - y if Y == 2 else 0
    scale = D ** (-0.5)
    GL = G // Y
    C = Y * T
    CP = Y * (T + PAD)
    HT = H * T
    Q = Y * HT
    first = y * GL
    theirs = other * GL

    def at(zz, yy):
        return {"ctx": zz * Y + yy}

    inputs = [(k_hbm, k_ref), (q_hbm, q_ref), (v_hbm, v_ref), (do_hbm, do_ref), (fo_hbm, fo_ref)]
    loads = [pltpu.make_async_copy(a, b, in_sem.at[i]) for i, (a, b) in enumerate(inputs)]
    for cp in loads:
        cp.start()

    barrier = pltpu.get_barrier_semaphore()

    for d in range(1, Z):
        pl.semaphore_signal(
            barrier, inc=1, device_id=at(lax.rem(z + d, Z), y), device_id_type=MESH)
    if Y == 2:
        pl.semaphore_signal(barrier, inc=1, device_id=at(z, other), device_id_type=MESH)

    def head(src, heads, h):
        return tmp[pl.ds(h, T, stride=heads), :]

    def aligned(x):
        return pl.multiple_of(x, 16)

    def ycopy(i, src, dst):
        return pltpu.make_async_remote_copy(
            src_ref=src, dst_ref=dst, send_sem=ys.at[i], recv_sem=yr.at[i],
            device_id=at(z, other), device_id_type=MESH)

    own_rows = pl.ds(aligned(y * HT), HT)
    own_keys = pl.ds(aligned(y * (T + PAD)), T + PAD)
    own_vals = pl.ds(aligned(y * T), T)
    own_lanes = pl.ds(pl.multiple_of(y * HT, 128), HT)
    y_copies = []
    if Y == 2:
        y_copies = [
            ycopy(0, kst, kbuf.at[z, :, own_keys]),
            ycopy(1, qst, qs.at[:, own_rows]),
            ycopy(2, vst, vbuf.at[z, :, own_vals]),
            ycopy(3, dost, dos.at[:, own_rows]),
            ycopy(4, delst, delta.at[:, :, own_lanes]),
            ycopy(5, dqst, dqr),
            ycopy(6, gst.at[0], gr.at[0]),
            ycopy(7, gst.at[1], gr.at[1]),
        ]

    def y_start(i):
        if Y == 2:
            y_copies[i].start()

    def y_wait(i):
        if Y == 2:
            y_copies[i].wait_recv()

    def mate(i, near=True):
        if not near:
            i = Z - 2 - i
        up = i + jnp.where(i >= z, 1, 0)
        v = Z - 1 - i
        return jnp.where(z < Z // 2, up, v - jnp.where(v <= z, 1, 0))

    def ag_copy(buf, t, block, sems):
        return pltpu.make_async_remote_copy(
            src_ref=buf.at[block], dst_ref=buf.at[block],
            send_sem=sems[0].at[t], recv_sem=sems[1].at[block],
            device_id=at(t, y), device_id_type=MESH)

    def ag_send(buf, sems):
        loop(Z - 1, lambda i: ag_copy(buf, mate(i), z, sems).start())

    def ag_recv(buf, i, sems):
        ag_copy(buf, mate(i), mate(i), sems).wait_recv()

    k_sems = (ks_s, ks_r)
    v_sems = (vs_s, vs_r)

    own_off = off_ref[0].astype(F32)
    off_rows = jnp.full((PAD, D), own_off, F32).astype(BF16)
    loads[0].wait()
    tmp[0:T * G, :] = k_ref[...].astype(F32)
    for i in range(GL):
        kbuf[z, i, pl.ds(aligned(y * (T + PAD)), T), :] = head(tmp, G, first + i).astype(BF16)
        kbuf[z, i, pl.ds(aligned(y * (T + PAD) + T), PAD), :] = off_rows
        if Y == 2:
            kst[i, 0:T, :] = head(tmp, G, theirs + i).astype(BF16)
            kst[i, T:T + PAD, :] = off_rows
    pl.semaphore_wait(barrier, Z - 1 + Y - 1)
    y_start(0)

    def split_queries(dst, stage):
        for i in range(GL):
            for h in range(H):
                if Y == 2:
                    stage[i, pl.ds(h * T, T), :] = head(tmp, G * H, (theirs + i) * H + h).astype(BF16)
                dst[i, pl.ds(aligned(y * HT + h * T), T), :] = (
                    head(tmp, G * H, (first + i) * H + h).astype(BF16))

    loads[1].wait()
    tmp[...] = q_ref[...].astype(F32)
    split_queries(qs, qst)
    y_start(1)
    y_wait(0)
    ag_send(kbuf, k_sems)

    loads[2].wait()
    tmp[0:T * G, :] = v_ref[...].astype(F32)
    for i in range(GL):
        vbuf[z, i, own_vals, :] = head(tmp, G, first + i).astype(BF16)
        if Y == 2:
            vst[i] = head(tmp, G, theirs + i).astype(BF16)
    y_start(2)
    loads[3].wait()
    tmp[...] = do_ref[...].astype(F32)
    split_queries(dos, dost)
    y_start(3)

    loads[4].wait()
    tmp[...] = do_ref[...].astype(F32) * fo_ref[...].astype(F32)
    for i in range(GL):
        for h in range(H):
            def lanes(g):
                return jnp.sum(head(tmp, G * H, g * H + h).T, axis=0, keepdims=True)
            delta[i, :, pl.ds(pl.multiple_of(y * HT + h * T, 128), T)] = lanes(first + i)
            if Y == 2:
                delst[i, :, pl.ds(h * T, T)] = lanes(theirs + i)
    y_start(4)

    def key_rows(c, g):
        return jnp.concatenate([kbuf[c, g, pl.ds(i * (T + PAD), T), :] for i in range(Y)], axis=0)

    def block_off(c, i):
        return kbuf[c, 0, pl.ds(i * (T + PAD) + T, PAD), :][0:1, :].astype(F32)

    lead = (lax.broadcasted_iota(jnp.int32, (T, Q), 0)
            - lax.broadcasted_iota(jnp.int32, (T, Q), 1) % T).astype(F32)
    top_scr[...] = jnp.full(top_scr.shape, -1e30, F32)
    y_wait(1)
    q_off = jnp.concatenate([block_off(z, i) for i in range(Y) for h in range(H)], axis=1)

    def scores(c):
        for g in range(GL):
            s = dot_nt(key_rows(c, g), qs[g]) * (scale * LOG2E)
            parts = []
            for i in range(Y):
                off = jnp.concatenate([block_off(c, i)] * (Q // D), axis=1)
                parts.append(jnp.where(lead <= (q_off - off) * T, s[i * T:(i + 1) * T], -1e30))
            s = jnp.concatenate(parts, axis=0)
            s_scr[g, pl.ds(pl.multiple_of(c * C, 128), C), :] = s
            top_scr[g] = jnp.maximum(top_scr[g], jnp.max(s.reshape(C // 8, 8, Q), axis=0))

    scores(z)
    y_wait(2)
    ag_send(vbuf, v_sems)

    def key_arrival(i):
        ag_recv(kbuf, i, k_sems)
        scores(mate(i))

    loop(Z - 1, key_arrival)

    tops = [jnp.max(top_scr[g], axis=0, keepdims=True) for g in range(GL)]

    def total_step(c, sums):
        new = []
        for g in range(GL):
            rows = pl.ds(pl.multiple_of(c * C, 128), C)
            e = jnp.exp2(s_scr[g, rows, :] - tops[g])
            s_scr[g, rows, :] = e
            new.append(sums[g] + jnp.sum(e.reshape(C // 8, 8, Q), axis=0))
        return tuple(new)

    sums = lax.fori_loop(0, Z, total_step, tuple(jnp.zeros((8, Q), F32) for _ in range(GL)))
    inv = [1.0 / jnp.sum(t, axis=0, keepdims=True) for t in sums]

    y_wait(3)

    def rs_copy(c, src, bufs, sems):
        return pltpu.make_async_remote_copy(
            src_ref=bufs[0].at[c], dst_ref=bufs[1].at[src],
            send_sem=sems[0].at[c], recv_sem=sems[1].at[src],
            device_id=at(c, y), device_id_type=MESH)

    bufs_v, sems_v = (gsv, grv), (gv_s, gv_r)
    bufs_k, sems_k = (gsk, grk), (gk_s, gk_r)

    def value_chunk(c, put):
        rows = pl.ds(pl.multiple_of(c * C, 128), C)
        for g in range(GL):
            p = s_scr[g, rows, :] * inv[g]
            s_scr[g, rows, :] = p
            put(g, dot_nn(p.astype(BF16), dos[g]))

    def key_chunk(c, put):
        rows = pl.ds(pl.multiple_of(c * C, 128), C)
        for g in range(GL):
            dp = dot_nt(vbuf[c, g], dos[g])
            ds = (s_scr[g, rows, :] * (dp - delta[g])).astype(BF16)
            ds_scr[g, rows, :] = ds
            put(g, dot_nn(ds, qs[g]) * scale)

    def send_chunk(i, chunk, bufs, sems):
        c = mate(i, False)

        def put(g, x):
            bufs[0][c, pl.ds(g * C, C), :] = x.astype(BF16)

        chunk(c, put)
        rs_copy(c, z, bufs, sems).start()

    def own_chunk(chunk, part):
        def put(g, x):
            part[pl.ds(g * C, C), :] = x

        chunk(z, put)

    loop(Z - 1, lambda i: send_chunk(i, value_chunk, bufs_v, sems_v))
    own_chunk(value_chunk, partv)
    y_wait(4)
    loop(Z - 1, lambda i: ag_recv(vbuf, i, v_sems))
    loop(Z - 1, lambda i: send_chunk(i, key_chunk, bufs_k, sems_k))
    own_chunk(key_chunk, partk)

    for g in range(GL):
        kt = jnp.concatenate(
            [key_rows(c, g).astype(F32).T.astype(BF16) for c in range(Z)], axis=1)
        dqt = dot_nn(kt, ds_scr[g]) * scale
        for i in range(Y):
            for h in range(H):
                block = dqt[:, (i * H + h) * T:(i * H + h + 1) * T].T

                def keep(block=block, h=h):
                    dq_ref[pl.ds((first + g) * H + h, T, stride=G * H), :] = block

                def stage(block=block, h=h):
                    dqst[g, pl.ds(h * T, T), :] = block.astype(BF16)

                if Y == 2:
                    pl.when(y == i)(keep)
                    pl.when(y != i)(stage)
                else:
                    keep()
    y_start(5)

    def finish(part, bufs, sems, slot):
        def add(i):
            rs_copy(z, mate(i), bufs, sems).wait_recv()
            part[...] += bufs[1][mate(i)].astype(F32)

        loop(Z - 1, add)
        if Y == 2:
            for g in range(GL):
                gst[slot, g] = part[pl.ds(aligned(g * C + other * T), T), :].astype(BF16)
        y_start(6 + slot)

    def put(out, part, slot):
        for g in range(GL):
            out[pl.ds(first + g, T, stride=G), :] = part[pl.ds(aligned(g * C + y * T), T), :]
        y_wait(6 + slot)
        if Y == 2:
            for g in range(GL):
                out[pl.ds(theirs + g, T, stride=G), :] = gr[slot, g].astype(F32)

    finish(partv, bufs_v, sems_v, 0)
    put(dv_ref, partv, 0)
    y_wait(5)
    if Y == 2:
        for g in range(GL):
            for h in range(H):
                dq_ref[pl.ds((theirs + g) * H + h, T, stride=G * H), :] = (
                    dqr[g, pl.ds(h * T, T), :].astype(F32))
    finish(partk, bufs_k, sems_k, 1)
    put(dk_ref, partk, 1)

    def drain(i):
        t = mate(i)
        ag_copy(kbuf, t, z, k_sems).wait_send()
        ag_copy(vbuf, t, z, v_sems).wait_send()
        rs_copy(t, z, bufs_v, sems_v).wait_send()
        rs_copy(t, z, bufs_k, sems_k).wait_send()

    loop(Z - 1, drain)
    for cp in y_copies:
        cp.wait_send()


def on_device(Y, query_vectors, key_vectors, value_rows, forward_out, out_grad, block_offsets):
    T, QH, D = query_vectors.shape
    G = key_vectors.shape[1]
    H = QH // G
    N = lax.axis_size("ctx")
    Z = N // Y
    GL, C, HT, R = G // Y, Y * T, H * T, T * G
    Q = Y * HT
    vmem = pl.BlockSpec(memory_space=pltpu.VMEM)
    smem = pl.BlockSpec(memory_space=pltpu.SMEM)
    hbm = pl.BlockSpec(memory_space=pltpu.HBM)
    V = pltpu.VMEM
    part = V((GL * C, D), F32)
    wire = V((Z, GL * C, D), BF16)
    dq, dk, dv = pl.pallas_call(
        functools.partial(kernel, Z, Y, G, H, T, D),
        out_shape=(
            jax.ShapeDtypeStruct((T * QH, D), F32),
            jax.ShapeDtypeStruct((R, D), F32),
            jax.ShapeDtypeStruct((R, D), F32),
        ),
        in_specs=[hbm] * 5 + [smem],
        out_specs=[vmem] * 3,
        scratch_shapes=[
            V((T * QH, D), BF16), V((R, D), BF16), V((R, D), BF16),
            V((T * QH, D), BF16), V((T * QH, D), BF16), pltpu.SemaphoreType.DMA((5,)),
            V((T * QH, D), F32),
            V((GL, Q, D), BF16), V((GL, Q, D), BF16),
            V((GL, HT, D), BF16), V((GL, HT, D), BF16),
            V((GL, T + PAD, D), BF16), V((GL, T, D), BF16),
            V((GL, 1, Q), F32), V((GL, 1, HT), F32),
            V((Z, GL, Y * (T + PAD), D), BF16), V((Z, GL, C, D), BF16),
            V((GL, N * T, Q), F32), V((GL, N * T, Q), BF16), V((GL, 8, Q), F32),
            part, part, wire, wire, wire, wire,
            V((GL, HT, D), BF16), V((GL, HT, D), BF16),
            V((2, GL, T, D), BF16), V((2, GL, T, D), BF16),
            pltpu.SemaphoreType.DMA((8,)), pltpu.SemaphoreType.DMA((8,)),
        ] + [pltpu.SemaphoreType.DMA((Z,))] * 8,
        compiler_params=pltpu.CompilerParams(
            collective_id=0, has_side_effects=True, vmem_limit_bytes=56 * 1024 * 1024
        ),
        cost_estimate=pl.CostEstimate(
            flops=10 * GL * Q * N * T * D, bytes_accessed=4 * T * QH * D * 4,
            transcendentals=GL * Q * N * T,
        ),
    )(
        query_vectors.reshape(T * QH, D), key_vectors.reshape(R, D), value_rows.reshape(R, D),
        forward_out.reshape(T * QH, D), out_grad.reshape(T * QH, D), block_offsets,
    )
    return dq.reshape(T, QH, D), dk.reshape(T, G, D), dv.reshape(T, G, D)


def solution(mesh):
    pair = 2 if mesh.shape["groups"] == 2 and mesh.shape["ctx"] % 2 == 0 else 1
    tokens = P(("groups", "ctx"), "heads", None)
    return jax.shard_map(
        functools.partial(on_device, pair), mesh=mesh,
        in_specs=(tokens,) * 5 + (P(("groups", "ctx")),),
        out_specs=(tokens,) * 3, check_vma=False,
    )
```

profile of v0, /device:TPU:0, one launch (start us, length us, event | category | flops | bytes accessed | tf_op | source)
XLA Modules:
  0.0 40.2 jit_solution(12133871236379756790)
XLA Ops:
  1.3 35.4 %shard_map.85 = (f32[1024,128]{1,0:T(8,128)}, f32[256,128]{1,0:T(8,128)}, f32[256,128]{1,0:T(8,128)}) custom-call(bf16[1024,128]{1,0:T(8,128)(2,1)} %bitcast.11, bf16[256,128]{1,0:T(8,128)(2,1)} %bitcast.14, bf16[256,128]{1,0:T(8,128)(2,1)} %bitcast.15, bf16[1024,128]{1,0:T(8,128)(2,1)} %bitcast.12, bf16[1024,128]{1,0:T(8,128)(2,1)} %bitcast.13, ...), custom_call_target="tpu_custom_call" | custom-call | flops 1342177280 | bytes 2097152 | tf_op jit(solution)/shard_map/pallas_call | solution.py:353
  36.7 0.0 copy-start.1
  36.7 1.9 %copy.13 = f32[128,8,128]{2,1,0:T(8,128)} copy(f32[128,8,128]{2,1,0:T(8,128)} %bitcast.8) | data formatting | bytes 1048576
  38.6 0.0 copy-done.1
  38.6 0.0 copy-start
  38.6 0.7 %copy.14 = f32[128,2,128]{2,1,0:T(2,128)} copy(f32[128,2,128]{2,1,0:T(2,128)S(1)} %bitcast.10) | data formatting | bytes 262144
  39.3 0.3 copy-done
  39.5 0.7 %copy.15 = f32[128,2,128]{2,1,0:T(2,128)} copy(f32[128,2,128]{2,1,0:T(2,128)S(1)} %bitcast.9) | data formatting | bytes 262144
Async XLA Ops:
  36.7 1.9 %copy-start.1 = (f32[256,128]{1,0:T(8,128)S(1)}, f32[256,128]{1,0:T(8,128)}, u32[]{:S(2)}) copy-start(f32[256,128]{1,0:T(8,128)} %get-tuple-element.7) | copy-start | bytes 393220
  38.6 1.0 %copy-start = (f32[256,128]{1,0:T(8,128)S(1)}, f32[256,128]{1,0:T(8,128)}, u32[]{:S(2)}) copy-start(f32[256,128]{1,0:T(8,128)} %get-tuple-element.8) | copy-start | bytes 393220
where the time goes:
time: 40.4 us; the launch traced here: 40.2 us
  Pallas kernels  35.4 us (88%)
  local copies, waits for them, and re-layouts  3.51 us (9%)
  between operations  1.3 us (3%)
    pallas_call x1, Pallas kernels, on_device(): pl.pallas_call(functools.partial(kernel, Z, Y, G, H, T, D), out_shape=(ja...  35.4 us
    unnamed x7, local copies, waits for them, and re-layouts  3.51 us

commit v1 on v0

--- a/solution.py
+++ b/solution.py
@@ -37,9 +37,9 @@
     (q_hbm, k_hbm, v_hbm, fo_hbm, do_hbm, off_ref, dq_ref, dk_ref, dv_ref,
      q_ref, k_ref, v_ref, fo_ref, do_ref, in_sem,
      tmp, qs, dos, qst, dost, kst, vst, delta, delst, kbuf, vbuf,
-     s_scr, ds_scr, top_scr, partv, partk,
-     gsv, grv, gsk, grk,
-     dqst, dqr, gst, gr, ys, yr,
+     s_scr, ds_scr, top_scr,
+     gsv, grv, gsk, grk, ownv, ownk, midv, midk, viav, viak,
+     dqst, dqr, ys, yr, viav_s, viav_r, viak_s, viak_r,
      ks_s, ks_r, vs_s, vs_r, gv_s, gv_r, gk_s, gk_r) = refs
     me = lax.axis_index("ctx")
     z, y = me // Y, me % Y
@@ -49,6 +49,7 @@
     C = Y * T
     CP = Y * (T + PAD)
     HT = H * T
+    N = Z * Y
     Q = Y * HT
     first = y * GL
     theirs = other * GL
@@ -63,11 +64,10 @@
 
     barrier = pltpu.get_barrier_semaphore()
 
-    for d in range(1, Z):
-        pl.semaphore_signal(
-            barrier, inc=1, device_id=at(lax.rem(z + d, Z), y), device_id_type=MESH)
-    if Y == 2:
-        pl.semaphore_signal(barrier, inc=1, device_id=at(z, other), device_id_type=MESH)
+    for d in range(Z):
+        for yy in ([y] if d else []) + ([other] if Y == 2 else []):
+            pl.semaphore_signal(
+                barrier, inc=1, device_id=at(lax.rem(z + d, Z), yy), device_id_type=MESH)
 
     def head(src, heads, h):
         return tmp[pl.ds(h, T, stride=heads), :]
@@ -93,8 +93,6 @@
             ycopy(3, dost, dos.at[:, own_rows]),
             ycopy(4, delst, delta.at[:, :, own_lanes]),
             ycopy(5, dqst, dqr),
-            ycopy(6, gst.at[0], gr.at[0]),
-            ycopy(7, gst.at[1], gr.at[1]),
         ]
 
     def y_start(i):
@@ -118,11 +116,39 @@
             send_sem=sems[0].at[t], recv_sem=sems[1].at[block],
             device_id=at(t, y), device_id_type=MESH)
 
+    relayed = Z == 4
+    middle = (z > 0) & (z < Z - 1)
+
     def ag_send(buf, sems):
-        loop(Z - 1, lambda i: ag_copy(buf, mate(i), z, sems).start())
+        if not relayed:
+            loop(Z - 1, lambda i: ag_copy(buf, mate(i), z, sems).start())
+            return
+        pl.when(middle)(lambda: ag_copy(buf, mate(2), z, sems).start())
+        ag_copy(buf, mate(1), z, sems).start()
+        ag_copy(buf, mate(0), z, sems).start()
+
+    def ag_relay(buf, sems):
+        return pltpu.make_async_remote_copy(
+            src_ref=buf.at[mate(2)], dst_ref=buf.at[mate(2)],
+            send_sem=sems[0].at[z], recv_sem=sems[1].at[mate(2)],
+            device_id=at(Z - 1 - mate(2), y), device_id_type=MESH)
+
+    def arrival(i):
+        if not relayed or i == 0:
+            return mate(i)
+        return mate(jnp.where(middle, 3 - i, i))
 
     def ag_recv(buf, i, sems):
-        ag_copy(buf, mate(i), mate(i), sems).wait_recv()
+        ag_copy(buf, arrival(i), arrival(i), sems).wait_recv()
+        if relayed and i == 1:
+            pl.when(middle)(lambda: ag_relay(buf, sems).start())
+
+    def ag_drain(buf, i, sems):
+        if not relayed or i < 2:
+            ag_copy(buf, mate(i), z, sems).wait_send()
+            return
+        pl.when(middle)(lambda: ag_copy(buf, mate(2), z, sems).wait_send())
+        pl.when(middle)(lambda: ag_relay(buf, sems).wait_send())
 
     k_sems = (ks_s, ks_r)
     v_sems = (vs_s, vs_r)
@@ -137,7 +163,7 @@
         if Y == 2:
             kst[i, 0:T, :] = head(tmp, G, theirs + i).astype(BF16)
             kst[i, T:T + PAD, :] = off_rows
-    pl.semaphore_wait(barrier, Z - 1 + Y - 1)
+    pl.semaphore_wait(barrier, N - 1)
     y_start(0)
 
     def split_queries(dst, stage):
@@ -207,7 +233,7 @@
 
     def key_arrival(i):
         ag_recv(kbuf, i, k_sems)
-        scores(mate(i))
+        scores(arrival(i))
 
     loop(Z - 1, key_arrival)
 
@@ -227,14 +253,35 @@
 
     y_wait(3)
 
-    def rs_copy(c, src, bufs, sems):
-        return pltpu.make_async_remote_copy(
-            src_ref=bufs[0].at[c], dst_ref=bufs[1].at[src],
-            send_sem=sems[0].at[c], recv_sem=sems[1].at[src],
-            device_id=at(c, y), device_id_type=MESH)
-
-    bufs_v, sems_v = (gsv, grv), (gv_s, gv_r)
-    bufs_k, sems_k = (gsk, grk), (gk_s, gk_r)
+    class Sums:
+        def __init__(self, send, recv, own, mid, via, ss, rs, via_s, via_r):
+            self.send, self.recv, self.own, self.mid, self.via = send, recv, own, mid, via
+            self.ss, self.rs, self.via_s, self.via_r = ss, rs, via_s, via_r
+
+        def copy(self, c, half):
+            return pltpu.make_async_remote_copy(
+                src_ref=self.send.at[c, half], dst_ref=self.recv.at[z, y],
+                send_sem=self.ss.at[c, half], recv_sem=self.rs.at[z, y],
+                device_id=at(c, half), device_id_type=MESH)
+
+        def arrive(self, src_z, src_y):
+            pltpu.make_async_remote_copy(
+                src_ref=self.send.at[z, y], dst_ref=self.recv.at[src_z, src_y],
+                send_sem=self.ss.at[z, y], recv_sem=self.rs.at[src_z, src_y],
+                device_id=at(lax.rem(z + 1, Z), y), device_id_type=MESH).wait_recv()
+
+        def to_middle(self):
+            return pltpu.make_async_remote_copy(
+                src_ref=self.send.at[mate(Z - 2)], dst_ref=self.via,
+                send_sem=self.via_s, recv_sem=self.via_r,
+                device_id=at(mate(0), y), device_id_type=MESH)
+
+        def start(self, c):
+            for half in range(Y):
+                self.copy(c, half).start()
+
+    sum_v = Sums(gsv, grv, ownv, midv, viav, gv_s, gv_r, viav_s, viav_r)
+    sum_k = Sums(gsk, grk, ownk, midk, viak, gk_s, gk_r, viak_s, viak_r)
 
     def value_chunk(c, put):
         rows = pl.ds(pl.multiple_of(c * C, 128), C)
@@ -251,27 +298,59 @@
             ds_scr[g, rows, :] = ds
             put(g, dot_nn(ds, qs[g]) * scale)
 
-    def send_chunk(i, chunk, bufs, sems):
-        c = mate(i, False)
-
+    def putter(ref):
         def put(g, x):
-            bufs[0][c, pl.ds(g * C, C), :] = x.astype(BF16)
-
-        chunk(c, put)
-        rs_copy(c, z, bufs, sems).start()
-
-    def own_chunk(chunk, part):
-        def put(g, x):
-            part[pl.ds(g * C, C), :] = x
-
-        chunk(z, put)
-
-    loop(Z - 1, lambda i: send_chunk(i, value_chunk, bufs_v, sems_v))
-    own_chunk(value_chunk, partv)
+            for half in range(Y):
+                ref[half, pl.ds(g * T, T), :] = x[half * T:(half + 1) * T].astype(ref.dtype)
+        return put
+
+    def send_chunks(chunk, sums):
+        if not relayed:
+            def one(i):
+                c = mate(i, False)
+                chunk(c, putter(sums.send.at[c]))
+                sums.start(c)
+            loop(Z - 1, one)
+            return
+
+        @pl.when(jnp.logical_not(middle))
+        def _():
+            c = mate(2)
+            chunk(c, putter(sums.send.at[c]))
+            sums.to_middle().start()
+
+        for i in (1, 0):
+            c = mate(i)
+            chunk(c, putter(sums.send.at[c]))
+            sums.start(c)
+        pl.when(middle)(lambda: chunk(mate(2), putter(sums.mid)))
+
+    def own_chunk(chunk, sums):
+        chunk(z, putter(sums.own))
+        if Y == 2:
+            sums.send[z, other] = sums.own[other].astype(BF16)
+            sums.copy(z, other).start()
+
+    def pass_on(sums):
+        if relayed:
+            @pl.when(middle)
+            def _():
+                c = mate(2)
+                sums.to_middle().wait_recv()
+                sums.send[c] = (sums.mid[...] + sums.via[...].astype(F32)).astype(BF16)
+                sums.start(c)
+
+    send_chunks(value_chunk, sum_v)
+    own_chunk(value_chunk, sum_v)
     y_wait(4)
-    loop(Z - 1, lambda i: ag_recv(vbuf, i, v_sems))
-    loop(Z - 1, lambda i: send_chunk(i, key_chunk, bufs_k, sems_k))
-    own_chunk(key_chunk, partk)
+    ag_recv(vbuf, 0, v_sems)
+    if Z > 2:
+        ag_recv(vbuf, 1, v_sems)
+    pass_on(sum_v)
+    loop(Z - 3, lambda i: ag_recv(vbuf, i + 2, v_sems))
+    send_chunks(key_chunk, sum_k)
+    own_chunk(key_chunk, sum_k)
+    pass_on(sum_k)
 
     for g in range(GL):
         kt = jnp.concatenate(
@@ -294,44 +373,56 @@
                     keep()
     y_start(5)
 
-    def finish(part, bufs, sems, slot):
+    def finish(out, sums):
+        def add_from(src):
+            sums.arrive(src, y)
+            sums.own[y] = sums.own[y] + sums.recv[src, y].astype(F32)
+            if Y == 2:
+                sums.arrive(src, other)
+                sums.own[other] = sums.own[other] + sums.recv[src, other].astype(F32)
+
         def add(i):
-            rs_copy(z, mate(i), bufs, sems).wait_recv()
-            part[...] += bufs[1][mate(i)].astype(F32)
-
+            if relayed and i == 2:
+                pl.when(middle)(lambda: add_from(mate(i)))
+            else:
+                add_from(mate(i))
+
+        if Y == 2:
+            sums.arrive(z, other)
+            sums.own[other] = sums.recv[z, other].astype(F32)
         loop(Z - 1, add)
-        if Y == 2:
-            for g in range(GL):
-                gst[slot, g] = part[pl.ds(aligned(g * C + other * T), T), :].astype(BF16)
-        y_start(6 + slot)
-
-    def put(out, part, slot):
-        for g in range(GL):
-            out[pl.ds(first + g, T, stride=G), :] = part[pl.ds(aligned(g * C + y * T), T), :]
-        y_wait(6 + slot)
-        if Y == 2:
-            for g in range(GL):
-                out[pl.ds(theirs + g, T, stride=G), :] = gr[slot, g].astype(F32)
-
-    finish(partv, bufs_v, sems_v, 0)
-    put(dv_ref, partv, 0)
+        for g in range(GL):
+            out[pl.ds(first + g, T, stride=G), :] = sums.own[y, pl.ds(g * T, T), :]
+            if Y == 2:
+                out[pl.ds(theirs + g, T, stride=G), :] = sums.own[other, pl.ds(g * T, T), :]
+
+    finish(dv_ref, sum_v)
     y_wait(5)
     if Y == 2:
         for g in range(GL):
             for h in range(H):
                 dq_ref[pl.ds((theirs + g) * H + h, T, stride=G * H), :] = (
                     dqr[g, pl.ds(h * T, T), :].astype(F32))
-    finish(partk, bufs_k, sems_k, 1)
-    put(dk_ref, partk, 1)
+    finish(dk_ref, sum_k)
 
     def drain(i):
-        t = mate(i)
-        ag_copy(kbuf, t, z, k_sems).wait_send()
-        ag_copy(vbuf, t, z, v_sems).wait_send()
-        rs_copy(t, z, bufs_v, sems_v).wait_send()
-        rs_copy(t, z, bufs_k, sems_k).wait_send()
+        ag_drain(kbuf, i, k_sems)
+        ag_drain(vbuf, i, v_sems)
+        for sums in (sum_v, sum_k):
+            def direct(sums=sums):
+                for half in range(Y):
+                    sums.copy(mate(i), half).wait_send()
+
+            if relayed and i == 2:
+                pl.when(middle)(direct)
+                pl.when(jnp.logical_not(middle))(sums.to_middle().wait_send)
+            else:
+                direct()
 
     loop(Z - 1, drain)
+    if Y == 2:
+        sum_v.copy(z, other).wait_send()
+        sum_k.copy(z, other).wait_send()
     for cp in y_copies:
         cp.wait_send()
 
@@ -348,8 +439,8 @@
     smem = pl.BlockSpec(memory_space=pltpu.SMEM)
     hbm = pl.BlockSpec(memory_space=pltpu.HBM)
     V = pltpu.VMEM
-    part = V((GL * C, D), F32)
-    wire = V((Z, GL * C, D), BF16)
+    own = V((Y, GL * T, D), F32)
+    wire = V((Z, Y, GL * T, D), BF16)
     dq, dk, dv = pl.pallas_call(
         functools.partial(kernel, Z, Y, G, H, T, D),
         out_shape=(
@@ -369,11 +460,11 @@
             V((GL, 1, Q), F32), V((GL, 1, HT), F32),
             V((Z, GL, Y * (T + PAD), D), BF16), V((Z, GL, C, D), BF16),
             V((GL, N * T, Q), F32), V((GL, N * T, Q), BF16), V((GL, 8, Q), F32),
-            part, part, wire, wire, wire, wire,
+            wire, wire, wire, wire, own, own, own, own, V((Y, GL * T, D), BF16), V((Y, GL * T, D), BF16),
             V((GL, HT, D), BF16), V((GL, HT, D), BF16),
-            V((2, GL, T, D), BF16), V((2, GL, T, D), BF16),
-            pltpu.SemaphoreType.DMA((8,)), pltpu.SemaphoreType.DMA((8,)),
-        ] + [pltpu.SemaphoreType.DMA((Z,))] * 8,
+            pltpu.SemaphoreType.DMA((6,)), pltpu.SemaphoreType.DMA((6,)),
+        ] + [pltpu.SemaphoreType.DMA] * 4 + [pltpu.SemaphoreType.DMA((Z,))] * 4
+        + [pltpu.SemaphoreType.DMA((Z, Y))] * 4,
         compiler_params=pltpu.CompilerParams(
             collective_id=0, has_side_effects=True, vmem_limit_bytes=56 * 1024 * 1024
         ),

time: 40.4 us -> 37.2 us (0.921)
  Pallas kernels: 35.4 us -> 32.2 us
    pallas_call x1, Pallas kernels: 35.4 us -> 32.2 us  [on_device(): pl.pallas_call(functools.partial(kernel, Z, Y, G, H, T, D), out_shape=(ja...]
where the time goes in v1:
time: 37.2 us; the launch traced here: 37 us
  Pallas kernels  32.2 us (87%)
  local copies, waits for them, and re-layouts  3.51 us (9%)
  between operations  1.3 us (3%)
    pallas_call x1, Pallas kernels, on_device(): pl.pallas_call(functools.partial(kernel, Z, Y, G, H, T, D), out_shape=(ja...  32.2 us
    unnamed x7, local copies, waits for them, and re-layouts  3.51 us

profile of v1, /device:TPU:0, one launch (start us, length us, event | category | flops | bytes accessed | tf_op | source)
XLA Modules:
  0.0 37.0 jit_solution(544157374766222245)
XLA Ops:
  1.3 32.2 %shard_map.85 = (f32[1024,128]{1,0:T(8,128)}, f32[256,128]{1,0:T(8,128)}, f32[256,128]{1,0:T(8,128)}) custom-call(bf16[1024,128]{1,0:T(8,128)(2,1)} %bitcast.11, bf16[256,128]{1,0:T(8,128)(2,1)} %bitcast.14, bf16[256,128]{1,0:T(8,128)(2,1)} %bitcast.15, bf16[1024,128]{1,0:T(8,128)(2,1)} %bitcast.12, bf16[1024,128]{1,0:T(8,128)(2,1)} %bitcast.13, ...), custom_call_target="tpu_custom_call" | custom-call | flops 1342177280 | bytes 2097152 | tf_op jit(solution)/shard_map/pallas_call | solution.py:444
  33.5 0.0 copy-start.1
  33.5 1.9 %copy.13 = f32[128,8,128]{2,1,0:T(8,128)} copy(f32[128,8,128]{2,1,0:T(8,128)} %bitcast.8) | data formatting | bytes 1048576
  35.4 0.0 copy-done.1
  35.4 0.0 copy-start
  35.4 0.7 %copy.14 = f32[128,2,128]{2,1,0:T(2,128)} copy(f32[128,2,128]{2,1,0:T(2,128)S(1)} %bitcast.10) | data formatting | bytes 262144
  36.1 0.3 copy-done
  36.4 0.7 %copy.15 = f32[128,2,128]{2,1,0:T(2,128)} copy(f32[128,2,128]{2,1,0:T(2,128)S(1)} %bitcast.9) | data formatting | bytes 262144
Async XLA Ops:
  33.5 1.9 %copy-start.1 = (f32[256,128]{1,0:T(8,128)S(1)}, f32[256,128]{1,0:T(8,128)}, u32[]{:S(2)}) copy-start(f32[256,128]{1,0:T(8,128)} %get-tuple-element.7) | copy-start | bytes 393220
  35.4 1.0 %copy-start = (f32[256,128]{1,0:T(8,128)S(1)}, f32[256,128]{1,0:T(8,128)}, u32[]{:S(2)}) copy-start(f32[256,128]{1,0:T(8,128)} %get-tuple-element.8) | copy-start | bytes 393220
